TPU v7x, 32 devices: a whole 2x2x4 slice. The times are simulated.
32 devices in a mesh: row: 4 (over y, core), col: 4 (over z), tm: 2 (over x).
Axes of the slice: x: 2, y: 2, z: 4, core: 2. Of those that a mesh axis runs over, the one named last changes fastest.
Arguments:
- counts: float32 [1024, 256, 512], P('row', 'col', 'tm'), may hold values from 0 to 60, as said below
- factor_a: float32 [1024, 32], P('row'), may hold values from 0.05 to 1
- factor_b: float32 [256, 32], P(('col', 'tm')), may hold values from 0.05 to 3, as said below
- factor_c: float32 [512, 32], P('tm'), may hold values from 0.1 to 1
Outputs:
- updated_a: float32 [1024, 32], P(('row', 'col', 'tm'))
Inputs may be any that keep to these rules, and one draw needn't show every extreme that they name: `counts`: whole numbers. `factor_b`: positive.
All inputs are finite; a program needn't handle non-finite values.
Results may differ from a plain program's by a relative error of at most 0.00027.
Values sent between devices are 32-bit elements; how exact they have to be, the bound alone decides.
A program may use at most 128 MiB of HBM per device.

v0:
```python
import functools

import jax
import jax.numpy as jnp
from jax import lax
from jax.experimental import pallas as pl
from jax.experimental.pallas import tpu as pltpu
from jax.sharding import PartitionSpec as P

ITERS = 6
MESH = pl.DeviceIdType.MESH
BF16 = jnp.bfloat16
F32 = jnp.float32


def kernel(
    cols, tms, blocks, rows,
    counts_hbm, a_ref, b_ref, c_ref, out_ref,
    counts_v, cur, part, recv, sums, b_all, norm_b, c_in, c_out,
    counts_sem, sums_send, sums_recv, b_send, b_recv,
    rs_send, rs_recv, ag_send, ag_recv,
):
    group = cols * tms
    my_col, my_tm = lax.axis_index("col"), lax.axis_index("tm")
    me = my_col * tms + my_tm
    rank = a_ref.shape[1]
    copies = 128 // rank
    j_own = b_ref.shape[0]
    j_local = j_own * tms
    k_local = c_ref.shape[0]
    whole_j = j_local * cols
    whole_k = k_local * tms
    cells = float(whole_j * whole_k)

    def peer(d):
        return lax.rem(me + d, group)

    def device(p):
        return {"col": lax.div(p, tms), "tm": lax.rem(p, tms)}

    def load(b):
        return pltpu.make_async_copy(
            counts_hbm.at[:, b], counts_v.at[:, b], counts_sem.at[b]
        )

    for b in range(blocks):
        load(b).start()

    barrier = pltpu.get_barrier_semaphore()
    for d in range(1, group):
        pl.semaphore_signal(barrier, inc=1, device_id=device(peer(d)), device_id_type=MESH)

    b_wide = jnp.concatenate([b_ref[...]] * copies, axis=1)
    c_wide = jnp.concatenate([c_ref[...]] * copies, axis=1)
    b_sum = jnp.sum(b_wide, axis=0, keepdims=True)
    c_sum = jnp.sum(c_wide, axis=0, keepdims=True)
    line = lax.broadcasted_iota(jnp.int32, (8, 128), 0)
    b_all[my_tm] = b_wide
    sums[me] = jnp.where(line == 0, b_sum, c_sum)
    a_wide = jnp.concatenate([a_ref[...]] * copies, axis=1)
    cur[...] = a_wide.reshape(cur.shape)

    pl.semaphore_wait(barrier, group - 1)

    def send_sums(p, q):
        return pltpu.make_async_remote_copy(
            src_ref=sums.at[q], dst_ref=sums.at[q],
            send_sem=sums_send.at[p], recv_sem=sums_recv.at[q],
            device_id=device(p), device_id_type=MESH,
        )

    def send_b(t, owner):
        return pltpu.make_async_remote_copy(
            src_ref=b_all.at[owner], dst_ref=b_all.at[owner],
            send_sem=b_send.at[t], recv_sem=b_recv.at[owner],
            device_id={"tm": t}, device_id_type=MESH,
        )

    for d in range(1, group):
        send_sums(peer(d), me).start()
    for d in range(1, tms):
        send_b(lax.rem(my_tm + d, tms), my_tm).start()
    for d in range(1, group):
        send_sums(peer(d), peer(d)).wait_recv()
    for d in range(1, tms):
        other = lax.rem(my_tm + d, tms)
        send_b(other, other).wait_recv()

    all_sums = jnp.sum(sums[...], axis=0)
    sum_b = all_sums[0:1]
    sum_c = all_sums[1:2] / cols
    norm_b[...] = b_all[...].reshape(j_local, 128) / (sum_b / whole_j)
    c_norm = c_wide / (sum_c / whole_k)
    c_high = c_norm.astype(BF16).astype(F32)
    c_low = c_norm - c_high
    lane = lax.broadcasted_iota(jnp.int32, (k_local, 128), 1) // rank
    mixed = jnp.where(lane % 2 == 0, c_high, c_low)
    c_in[...] = mixed.T.astype(BF16)
    once = jnp.where(lane < 2, mixed, 0.0).astype(BF16)
    c_out[0:k_local] = once
    c_out[k_local : 2 * k_local] = once

    for d in range(1, group):
        send_sums(peer(d), me).wait_send()
    for d in range(1, tms):
        send_b(lax.rem(my_tm + d, tms), my_tm).wait_send()

    def send_part(p, q, b):
        return pltpu.make_async_remote_copy(
            src_ref=part.at[p, b], dst_ref=recv.at[q, b],
            send_sem=rs_send.at[p, b], recv_sem=rs_recv.at[q, b],
            device_id=device(p), device_id_type=MESH,
        )

    def send_cur(p, q, b):
        return pltpu.make_async_remote_copy(
            src_ref=cur.at[q, b], dst_ref=cur.at[q, b],
            send_sem=ag_send.at[p, b], recv_sem=ag_recv.at[q, b],
            device_id=device(p), device_id_type=MESH,
        )

    def chunk(p, b):
        weights = norm_b[...]
        first = cur[p, b][:, None, :] * weights[None]
        first = first.reshape(rows * j_local, 128)
        high = first.astype(BF16).astype(F32)
        lanes = lax.broadcasted_iota(jnp.int32, first.shape, 1)
        left = jnp.where(lanes < 2 * rank, first, first - high).astype(BF16)
        model = jnp.dot(left, c_in[...], preferred_element_type=F32)
        x = counts_v[p, b].reshape(rows * j_local, k_local)
        inverse = pl.reciprocal(model, approx=True)
        ratio_high = (x * inverse).astype(BF16)
        ratio_low = ((x - model * ratio_high.astype(F32)) * inverse).astype(BF16)
        ratio = jnp.concatenate([ratio_high, ratio_low], axis=1)
        inner = jnp.dot(ratio, c_out[...], preferred_element_type=F32)
        inner = inner.reshape(rows, j_local, 128) * weights[None]
        part[p, b] = jnp.sum(inner, axis=1)

    def finish(u):
        b = lax.rem(u, blocks)
        for d in range(1, group):
            send_part(peer(d), peer(d), b).wait_recv()

        @pl.when(u >= blocks)
        def _():
            for d in range(1, group):
                send_cur(peer(d), me, b).wait_send()

        total = part[me, b]
        for d in range(1, group):
            total = total + recv[peer(d), b]
        width = 64
        while width >= rank:
            total = total + pltpu.roll(total, width, 1)
            width //= 2
        new = cur[me, b] * (total / cells)
        cur[me, b] = new

        @pl.when(u < (ITERS - 1) * blocks)
        def _():
            for d in range(1, group):
                send_cur(peer(d), me, b).start()

    lag = 1 if blocks > 1 else 0
    steps = ITERS * blocks

    def step(s, carry):
        b = lax.rem(s, blocks)

        @pl.when(s < blocks)
        def _():
            load(b).wait()

        @pl.when(s >= blocks)
        def _():
            for d in range(1, group):
                send_cur(peer(d), peer(d), b).wait_recv()
                send_part(peer(d), me, b).wait_send()

        def one(d, carry):
            p = peer(d)
            chunk(p, b)

            @pl.when(d < group)
            def _():
                send_part(p, me, b).start()

            return carry

        lax.fori_loop(1, group + 1, one, 0)

        @pl.when(s >= lag)
        def _():
            finish(s - lag)

        return carry

    lax.fori_loop(0, steps, step, 0)
    if lag:
        finish(steps - 1)
    for b in range(blocks):
        for d in range(1, group):
            send_part(peer(d), me, b).wait_send()
        out_ref[b * rows : (b + 1) * rows, :] = cur[me, b][:, 0:rank]


def per_device(counts, factor_a, factor_b, factor_c):
    cols, tms = lax.axis_size("col"), lax.axis_size("tm")
    group = cols * tms
    rows_local, j_local, k_local = counts.shape
    rank = factor_a.shape[1]
    own = rows_local // group
    rows = 8 if own % 8 == 0 else own
    blocks = own // rows
    counts = counts.reshape(group, blocks, rows, j_local, k_local)
    cells = rows_local * j_local * k_local
    vmem = pl.BlockSpec(memory_space=pltpu.VMEM)
    dma = pltpu.SemaphoreType.DMA
    return pl.pallas_call(
        functools.partial(kernel, cols, tms, blocks, rows),
        out_shape=jax.ShapeDtypeStruct((own, rank), F32),
        in_specs=[pl.BlockSpec(memory_space=pl.ANY), vmem, vmem, vmem],
        out_specs=vmem,
        scratch_shapes=[
            pltpu.VMEM(counts.shape, F32),
            pltpu.VMEM((group, blocks, rows, 128), F32),
            pltpu.VMEM((group, blocks, rows, 128), F32),
            pltpu.VMEM((group, blocks, rows, 128), F32),
            pltpu.VMEM((group, 8, 128), F32),
            pltpu.VMEM((tms, j_local // tms, 128), F32),
            pltpu.VMEM((j_local, 128), F32),
            pltpu.VMEM((128, k_local), BF16),
            pltpu.VMEM((2 * k_local, 128), BF16),
            dma((blocks,)),
            dma((group,)),
            dma((group,)),
            dma((tms,)),
            dma((tms,)),
            dma((group, blocks)),
            dma((group, blocks)),
            dma((group, blocks)),
            dma((group, blocks)),
        ],
        compiler_params=pltpu.CompilerParams(
            collective_id=0, has_side_effects=True, vmem_limit_bytes=48 * 1024 * 1024
        ),
        cost_estimate=pl.CostEstimate(
            flops=4 * ITERS * cells * rank,
            bytes_accessed=4 * cells,
            transcendentals=ITERS * cells,
        ),
    )(counts, factor_a, factor_b, factor_c)


def solution(mesh):
    return jax.shard_map(
        per_device,
        mesh=mesh,
        in_specs=(P("row", "col", "tm"), P("row", None), P(("col", "tm"), None), P("tm", None)),
        out_specs=P(("row", "col", "tm"), None),
        check_vma=False,
    )
```

profile of v0, /device:TPU:0, one launch (start us, length us, event | category | flops | bytes accessed | tf_op | source)
XLA Modules:
  0.0 123.2 jit_solution(11776038069126089708)
XLA Ops:
  0.0 0.9 copy.5.a_ref
  0.9 0.9 copy.6.c_ref
  1.7 0.0 copy-start
  1.7 0.7 copy-done
  2.4 120.1 %shard_map.46 = f32[32,32]{1,0:T(8,128)S(1)} custom-call(f32[8,4,8,64,256]{4,3,2,1,0:T(8,128)} %bitcast.1, f32[256,32]{1,0:T(8,128)S(1)} %copy.5.a_ref, f32[32,32]{1,0:T(8,128)S(1)} %copy-done, f32[256,32]{1,0:T(8,128)S(1)} %copy.6.c_ref), custom_call_target="tpu_custom_call" | custom-call | flops 3221225472 | bytes 16777216 | tf_op jit(solution)/shard_map/pallas_call | solution.py:219
  122.6 0.6 copy.8
Async XLA Ops:
  1.7 0.7 copy-start
where the time goes:
time: 123 us
  Pallas kernels  120 us (98%)
  local copies, waits for them, and re-layouts  3.03 us (2%)
    pallas_call x1, Pallas kernels, per_device(): pl.pallas_call(functools.partial(kernel, cols, tms, blocks, rows), out_sh...  120 us
    unnamed x5, local copies, waits for them, and re-layouts  3.03 us

commit v1 on v0

--- a/solution.py
+++ b/solution.py
@@ -14,7 +14,7 @@
 
 
 def kernel(
-    cols, tms, blocks, rows,
+    cols, tms, blocks, rows, pieces,
     counts_hbm, a_ref, b_ref, c_ref, out_ref,
     counts_v, cur, part, recv, sums, b_all, norm_b, c_in, c_out,
     counts_sem, sums_send, sums_recv, b_send, b_recv,
@@ -58,7 +58,10 @@
     b_all[my_tm] = b_wide
     sums[me] = jnp.where(line == 0, b_sum, c_sum)
     a_wide = jnp.concatenate([a_ref[...]] * copies, axis=1)
-    cur[...] = a_wide.reshape(cur.shape)
+    for p in range(group):
+        for b in range(blocks):
+            start = (p * blocks + b) * rows
+            cur[b, p] = a_wide[start : start + rows]
 
     pl.semaphore_wait(barrier, group - 1)
 
@@ -97,8 +100,7 @@
     mixed = jnp.where(lane % 2 == 0, c_high, c_low)
     c_in[...] = mixed.T.astype(BF16)
     once = jnp.where(lane < 2, mixed, 0.0).astype(BF16)
-    c_out[0:k_local] = once
-    c_out[k_local : 2 * k_local] = once
+    c_out[...] = once
 
     for d in range(1, group):
         send_sums(peer(d), me).wait_send()
@@ -107,61 +109,81 @@
 
     def send_part(p, q, b):
         return pltpu.make_async_remote_copy(
-            src_ref=part.at[p, b], dst_ref=recv.at[q, b],
-            send_sem=rs_send.at[p, b], recv_sem=rs_recv.at[q, b],
+            src_ref=part.at[b, p], dst_ref=recv.at[b, q],
+            send_sem=rs_send.at[b], recv_sem=rs_recv.at[b],
             device_id=device(p), device_id_type=MESH,
         )
 
     def send_cur(p, q, b):
         return pltpu.make_async_remote_copy(
-            src_ref=cur.at[q, b], dst_ref=cur.at[q, b],
-            send_sem=ag_send.at[p, b], recv_sem=ag_recv.at[q, b],
+            src_ref=cur.at[b, q], dst_ref=cur.at[b, q],
+            send_sem=ag_send.at[b], recv_sem=ag_recv.at[b],
             device_id=device(p), device_id_type=MESH,
         )
 
-    def chunk(p, b):
-        weights = norm_b[...]
-        first = cur[p, b][:, None, :] * weights[None]
-        first = first.reshape(rows * j_local, 128)
+    def wait_all(ref, sem, b):
+        pages = ref.at[b, pl.ds(0, group - 1)]
+        pltpu.make_async_copy(pages, pages, sem.at[b]).wait()
+
+    sub = rows // pieces
+    sub_rows = sub * j_local
+
+    def expand(p, b, h):
+        first = cur[b, p, h * sub : (h + 1) * sub][:, None, :] * norm_b[...][None]
+        first = first.reshape(sub_rows, 128)
         high = first.astype(BF16).astype(F32)
         lanes = lax.broadcasted_iota(jnp.int32, first.shape, 1)
         left = jnp.where(lanes < 2 * rank, first, first - high).astype(BF16)
-        model = jnp.dot(left, c_in[...], preferred_element_type=F32)
-        x = counts_v[p, b].reshape(rows * j_local, k_local)
+        return jnp.dot(left, c_in[...], preferred_element_type=F32)
+
+    def divide(p, b, h, model):
+        x = counts_v[p, b, h * sub : (h + 1) * sub].reshape(sub_rows, k_local)
         inverse = pl.reciprocal(model, approx=True)
         ratio_high = (x * inverse).astype(BF16)
         ratio_low = ((x - model * ratio_high.astype(F32)) * inverse).astype(BF16)
-        ratio = jnp.concatenate([ratio_high, ratio_low], axis=1)
-        inner = jnp.dot(ratio, c_out[...], preferred_element_type=F32)
-        inner = inner.reshape(rows, j_local, 128) * weights[None]
-        part[p, b] = jnp.sum(inner, axis=1)
+        return ratio_high, ratio_low
+
+    def collect(ratio_high, ratio_low):
+        split = []
+        for i in range(sub):
+            split += [ratio_high[i * j_local : (i + 1) * j_local]]
+            split += [ratio_low[i * j_local : (i + 1) * j_local]]
+        inner = jnp.dot(
+            jnp.concatenate(split, axis=0), c_out[...], preferred_element_type=F32
+        ).reshape(sub, 2, j_local, 128)
+        return jnp.sum((inner[:, 0] + inner[:, 1]) * norm_b[...][None], axis=1)
+
+    def chunk(p, b):
+        models = [expand(p, b, 0)]
+        sums_of = []
+        for h in range(pieces):
+            if h + 1 < pieces:
+                models.append(expand(p, b, h + 1))
+            sums_of.append(collect(*divide(p, b, h, models[h])))
+        part[b, p] = jnp.concatenate(sums_of, axis=0)
 
     def finish(u):
         b = lax.rem(u, blocks)
+        wait_all(recv, rs_recv, b)
+
+        @pl.when(u >= blocks)
+        def _():
+            wait_all(cur, ag_send, b)
+
+        total = part[b, me]
         for d in range(1, group):
-            send_part(peer(d), peer(d), b).wait_recv()
-
-        @pl.when(u >= blocks)
-        def _():
-            for d in range(1, group):
-                send_cur(peer(d), me, b).wait_send()
-
-        total = part[me, b]
-        for d in range(1, group):
-            total = total + recv[peer(d), b]
+            total = total + recv[b, peer(d)]
         width = 64
         while width >= rank:
             total = total + pltpu.roll(total, width, 1)
             width //= 2
-        new = cur[me, b] * (total / cells)
-        cur[me, b] = new
+        cur[b, me] = cur[b, me] * (total / cells)
 
         @pl.when(u < (ITERS - 1) * blocks)
         def _():
             for d in range(1, group):
                 send_cur(peer(d), me, b).start()
 
-    lag = 1 if blocks > 1 else 0
     steps = ITERS * blocks
 
     def step(s, carry):
@@ -173,9 +195,8 @@
 
         @pl.when(s >= blocks)
         def _():
-            for d in range(1, group):
-                send_cur(peer(d), peer(d), b).wait_recv()
-                send_part(peer(d), me, b).wait_send()
+            wait_all(cur, ag_recv, b)
+            wait_all(part, rs_send, b)
 
         def one(d, carry):
             p = peer(d)
@@ -187,21 +208,24 @@
 
             return carry
 
-        lax.fori_loop(1, group + 1, one, 0)
-
-        @pl.when(s >= lag)
-        def _():
-            finish(s - lag)
-
+        lax.fori_loop(1, group // 2 + 1, one, 0)
+        if blocks > 1:
+
+            @pl.when(s >= 1)
+            def _():
+                finish(s - 1)
+
+        lax.fori_loop(group // 2 + 1, group + 1, one, 0)
+        if blocks == 1:
+            finish(s)
         return carry
 
     lax.fori_loop(0, steps, step, 0)
-    if lag:
+    if blocks > 1:
         finish(steps - 1)
     for b in range(blocks):
-        for d in range(1, group):
-            send_part(peer(d), me, b).wait_send()
-        out_ref[b * rows : (b + 1) * rows, :] = cur[me, b][:, 0:rank]
+        wait_all(part, rs_send, b)
+        out_ref[b * rows : (b + 1) * rows, :] = cur[b, me][:, 0:rank]
 
 
 def per_device(counts, factor_a, factor_b, factor_c):
@@ -210,36 +234,37 @@
     rows_local, j_local, k_local = counts.shape
     rank = factor_a.shape[1]
     own = rows_local // group
-    rows = 8 if own % 8 == 0 else own
-    blocks = own // rows
+    blocks = 2 if own % 16 == 0 else 1
+    rows = own // blocks
+    pieces = max(1, rows // 4)
     counts = counts.reshape(group, blocks, rows, j_local, k_local)
     cells = rows_local * j_local * k_local
     vmem = pl.BlockSpec(memory_space=pltpu.VMEM)
     dma = pltpu.SemaphoreType.DMA
     return pl.pallas_call(
-        functools.partial(kernel, cols, tms, blocks, rows),
+        functools.partial(kernel, cols, tms, blocks, rows, pieces),
         out_shape=jax.ShapeDtypeStruct((own, rank), F32),
         in_specs=[pl.BlockSpec(memory_space=pl.ANY), vmem, vmem, vmem],
         out_specs=vmem,
         scratch_shapes=[
             pltpu.VMEM(counts.shape, F32),
-            pltpu.VMEM((group, blocks, rows, 128), F32),
-            pltpu.VMEM((group, blocks, rows, 128), F32),
-            pltpu.VMEM((group, blocks, rows, 128), F32),
+            pltpu.VMEM((blocks, group, rows, 128), F32),
+            pltpu.VMEM((blocks, group, rows, 128), F32),
+            pltpu.VMEM((blocks, group, rows, 128), F32),
             pltpu.VMEM((group, 8, 128), F32),
             pltpu.VMEM((tms, j_local // tms, 128), F32),
             pltpu.VMEM((j_local, 128), F32),
             pltpu.VMEM((128, k_local), BF16),
-            pltpu.VMEM((2 * k_local, 128), BF16),
+            pltpu.VMEM((k_local, 128), BF16),
             dma((blocks,)),
             dma((group,)),
             dma((group,)),
             dma((tms,)),
             dma((tms,)),
-            dma((group, blocks)),
-            dma((group, blocks)),
-            dma((group, blocks)),
-            dma((group, blocks)),
+            dma((blocks,)),
+            dma((blocks,)),
+            dma((blocks,)),
+            dma((blocks,)),
         ],
         compiler_params=pltpu.CompilerParams(
             collective_id=0, has_side_effects=True, vmem_limit_bytes=48 * 1024 * 1024

time: 123 us -> 99.1 us (0.81)
  Pallas kernels: 120 us -> 95.7 us
    pallas_call x1, Pallas kernels: 120 us -> 95.7 us  [per_device(): pl.pallas_call(functools.partial(kernel, cols, tms, blocks, rows, pieces)...]
where the time goes in v1:
time: 99.1 us; the launch traced here: 98.8 us
  Pallas kernels  95.7 us (97%)
  local copies, waits for them, and re-layouts  3.03 us (3%)
    pallas_call x1, Pallas kernels, per_device(): pl.pallas_call(functools.partial(kernel, cols, tms, blocks, rows, pieces)...  95.7 us
    unnamed x5, local copies, waits for them, and re-layouts  3.03 us

profile of v1, /device:TPU:0, one launch (start us, length us, event | category | flops | bytes accessed | tf_op | source)
XLA Modules:
  0.0 98.8 jit_solution(6806094053151379899)
XLA Ops:
  0.0 0.9 copy.5.a_ref
  0.9 0.9 copy.6.c_ref
  1.7 0.0 copy-start
  1.7 0.7 copy-done
  2.4 95.7 %shard_map.46 = f32[32,32]{1,0:T(8,128)S(1)} custom-call(f32[8,2,16,64,256]{4,3,2,1,0:T(8,128)} %bitcast.1, f32[256,32]{1,0:T(8,128)S(1)} %copy.5.a_ref, f32[32,32]{1,0:T(8,128)S(1)} %copy-done, f32[256,32]{1,0:T(8,128)S(1)} %copy.6.c_ref), custom_call_target="tpu_custom_call" | custom-call | flops 3221225472 | bytes 16777216 | tf_op jit(solution)/shard_map/pallas_call | solution.py:244
  98.2 0.6 copy.8
Async XLA Ops:
  1.7 0.7 copy-start

commit v2 on v1

--- a/solution.py
+++ b/solution.py
@@ -15,19 +15,20 @@
 
 def kernel(
     cols, tms, blocks, rows, pieces,
-    counts_hbm, a_ref, b_ref, c_ref, out_ref,
+    counts_hbm, a_hbm, b_hbm, c_hbm, out_ref,
+    a_ref, b_ref, c_ref,
     counts_v, cur, part, recv, sums, b_all, norm_b, c_in, c_out,
-    counts_sem, sums_send, sums_recv, b_send, b_recv,
+    factor_sem, counts_sem, sums_send, sums_recv, b_send, b_recv,
     rs_send, rs_recv, ag_send, ag_recv,
 ):
     group = cols * tms
     my_col, my_tm = lax.axis_index("col"), lax.axis_index("tm")
     me = my_col * tms + my_tm
-    rank = a_ref.shape[1]
+    rank = a_ref.shape[0]
     copies = 128 // rank
     j_own = b_ref.shape[0]
     j_local = j_own * tms
-    k_local = c_ref.shape[0]
+    k_local = c_ref.shape[1]
     whole_j = j_local * cols
     whole_k = k_local * tms
     cells = float(whole_j * whole_k)
@@ -43,6 +44,14 @@
             counts_hbm.at[:, b], counts_v.at[:, b], counts_sem.at[b]
         )
 
+    factors = [
+        pltpu.make_async_copy(source, target, factor_sem.at[i])
+        for i, (source, target) in enumerate(
+            [(b_hbm, b_ref), (c_hbm, c_ref), (a_hbm, a_ref)]
+        )
+    ]
+    for copy in factors:
+        copy.start()
     for b in range(blocks):
         load(b).start()
 
@@ -50,14 +59,16 @@
     for d in range(1, group):
         pl.semaphore_signal(barrier, inc=1, device_id=device(peer(d)), device_id_type=MESH)
 
+    for copy in factors:
+        copy.wait()
     b_wide = jnp.concatenate([b_ref[...]] * copies, axis=1)
-    c_wide = jnp.concatenate([c_ref[...]] * copies, axis=1)
+    c_wide = jnp.concatenate([c_ref[...]] * copies, axis=0).T
     b_sum = jnp.sum(b_wide, axis=0, keepdims=True)
     c_sum = jnp.sum(c_wide, axis=0, keepdims=True)
     line = lax.broadcasted_iota(jnp.int32, (8, 128), 0)
     b_all[my_tm] = b_wide
     sums[me] = jnp.where(line == 0, b_sum, c_sum)
-    a_wide = jnp.concatenate([a_ref[...]] * copies, axis=1)
+    a_wide = jnp.concatenate([a_ref[...]] * copies, axis=0).T
     for p in range(group):
         for b in range(blocks):
             start = (p * blocks + b) * rows
@@ -236,7 +247,7 @@
     own = rows_local // group
     blocks = 2 if own % 16 == 0 else 1
     rows = own // blocks
-    pieces = max(1, rows // 4)
+    pieces = max(1, rows // 8)
     counts = counts.reshape(group, blocks, rows, j_local, k_local)
     cells = rows_local * j_local * k_local
     vmem = pl.BlockSpec(memory_space=pltpu.VMEM)
@@ -244,9 +255,12 @@
     return pl.pallas_call(
         functools.partial(kernel, cols, tms, blocks, rows, pieces),
         out_shape=jax.ShapeDtypeStruct((own, rank), F32),
-        in_specs=[pl.BlockSpec(memory_space=pl.ANY), vmem, vmem, vmem],
+        in_specs=[pl.BlockSpec(memory_space=pltpu.HBM)] * 4,
         out_specs=vmem,
         scratch_shapes=[
+            pltpu.VMEM((rank, rows_local), F32),
+            pltpu.VMEM(factor_b.shape, F32),
+            pltpu.VMEM((rank, k_local), F32),
             pltpu.VMEM(counts.shape, F32),
             pltpu.VMEM((blocks, group, rows, 128), F32),
             pltpu.VMEM((blocks, group, rows, 128), F32),
@@ -256,6 +270,7 @@
             pltpu.VMEM((j_local, 128), F32),
             pltpu.VMEM((128, k_local), BF16),
             pltpu.VMEM((k_local, 128), BF16),
+            dma((3,)),
             dma((blocks,)),
             dma((group,)),
             dma((group,)),
@@ -274,7 +289,7 @@
             bytes_accessed=4 * cells,
             transcendentals=ITERS * cells,
         ),
-    )(counts, factor_a, factor_b, factor_c)
+    )(counts, factor_a.T, factor_b, factor_c.T)
 
 
 def solution(mesh):

time: 99.1 us -> 97.2 us (0.981)
  Pallas kernels: 95.7 us -> 94 us
    pallas_call x1, Pallas kernels: 95.7 us -> 94 us  [per_device(): pl.pallas_call(functools.partial(kernel, cols, tms, blocks, rows, pieces)...]
    unnamed x5 -> x7, local copies, waits for them, and re-layouts: 3.03 us -> 2.84 us
where the time goes in v2:
time: 97.2 us; the launch traced here: 96.9 us
  Pallas kernels  94 us (97%)
  local copies, waits for them, and re-layouts  2.84 us (3%)
    pallas_call x1, Pallas kernels, per_device(): pl.pallas_call(functools.partial(kernel, cols, tms, blocks, rows, pieces)...  94 us
    unnamed x7, local copies, waits for them, and re-layouts  2.84 us

profile of v2, /device:TPU:0, one launch (start us, length us, event | category | flops | bytes accessed | tf_op | source)
XLA Modules:
  0.0 96.9 jit_solution(7906316317442797469)
XLA Ops:
  0.0 0.0 copy-start
  0.0 0.8 copy-done
  0.8 0.0 copy-start.1
  0.8 0.8 copy-done.1
  1.5 0.0 copy-start.2
  1.5 0.7 copy-done.2
  2.2 94.0 %shard_map.46 = f32[32,32]{1,0:T(8,128)S(1)} custom-call(f32[8,2,16,64,256]{4,3,2,1,0:T(8,128)} %bitcast.5, f32[32,256]{1,0:T(8,128)S(1)} %bitcast.3, f32[32,32]{1,0:T(8,128)S(1)} %copy-done.2, f32[32,256]{1,0:T(8,128)S(1)} %bitcast.4), custom_call_target="tpu_custom_call" | custom-call | flops 3221225472 | bytes 16777216 | tf_op jit(solution)/shard_map/pallas_call | solution.py:255
  96.3 0.6 copy.6
Async XLA Ops:
  0.0 0.8 copy-start
  0.8 0.8 copy-start.1
  1.5 0.7 copy-start.2

commit v3 on v2

--- a/solution.py
+++ b/solution.py
@@ -247,7 +247,7 @@
     own = rows_local // group
     blocks = 2 if own % 16 == 0 else 1
     rows = own // blocks
-    pieces = max(1, rows // 8)
+    pieces = max(1, rows // 2)
     counts = counts.reshape(group, blocks, rows, j_local, k_local)
     cells = rows_local * j_local * k_local
     vmem = pl.BlockSpec(memory_space=pltpu.VMEM)

time: 97.2 us -> 105 us (1.080)
  Pallas kernels: 94 us -> 102 us
    pallas_call x1, Pallas kernels: 94 us -> 102 us  [per_device(): pl.pallas_call(functools.partial(kernel, cols, tms, blocks, rows, pieces)...]
where the time goes in v3:
time: 105 us; the launch traced here: 104 us
  Pallas kernels  102 us (97%)
  local copies, waits for them, and re-layouts  2.84 us (3%)
    pallas_call x1, Pallas kernels, per_device(): pl.pallas_call(functools.partial(kernel, cols, tms, blocks, rows, pieces)...  102 us
    unnamed x7, local copies, waits for them, and re-layouts  2.84 us

profile of v3, /device:TPU:0, one launch (start us, length us, event | category | flops | bytes accessed | tf_op | source)
XLA Modules:
  0.0 104.4 jit_solution(10257552677508401581)
XLA Ops:
  0.0 0.0 copy-start
  0.0 0.8 copy-done
  0.8 0.0 copy-start.1
  0.8 0.8 copy-done.1
  1.5 0.0 copy-start.2
  1.5 0.7 copy-done.2
  2.2 101.6 %shard_map.46 = f32[32,32]{1,0:T(8,128)S(1)} custom-call(f32[8,2,16,64,256]{4,3,2,1,0:T(8,128)} %bitcast.5, f32[32,256]{1,0:T(8,128)S(1)} %bitcast.3, f32[32,32]{1,0:T(8,128)S(1)} %copy-done.2, f32[32,256]{1,0:T(8,128)S(1)} %bitcast.4), custom_call_target="tpu_custom_call" | custom-call | flops 3221225472 | bytes 16777216 | tf_op jit(solution)/shard_map/pallas_call | solution.py:255
  103.8 0.6 copy.6
Async XLA Ops:
  0.0 0.8 copy-start
  0.8 0.8 copy-start.1
  1.5 0.7 copy-start.2
